TPU v7x, 256 devices: a whole 4x4x8 slice. The times are simulated.
256 devices in a mesh: sys: 4 (over y), blk: 32 (over x_lo, z, core), inst: 2 (over x_hi).
Axes of the slice: x: 4 (x_hi: 2, x_lo: 2; x = x_hi * 2 + x_lo), y: 4, z: 8, core: 2. Of those that a mesh axis runs over, the one named last changes fastest.
Arguments:
- adjoint: float32 [4, 8, 5, 512, 16, 128], P('sys', 'inst', None, 'blk'), may hold values from -6 to 6
- gradient: float32 [4, 8, 5, 512, 16, 128], P('sys', 'inst', None, 'blk'), may hold values from -6 to 6
- jacobian: float32 [4, 5, 5, 512, 16, 128], P('sys', None, None, 'blk'), may hold values from -3 to 3
- coupling: float32 [4, 6, 512, 16, 128], P('sys', None, 'blk'), may hold values from 0.1 to 0.6
- pseudo_step: float32 [4, 512, 16, 128], P('sys', 'blk'), may hold values from 0.2 to 1
- receptor_cell: int32 [4, 32, 1024], P('sys', 'blk'), may hold values from 0 to 32767
- donor_owner: int32 [4, 32, 1024, 1], P('sys', 'blk'), may hold values from 0 to 127; in each aligned block of 1024 rows (0 to 1023, 1024 to 2047, ..., all dimensions but the last counted through in order) at most 16 rows name the same one
- donor_cell: int32 [4, 32, 8, 1024], P('sys', 'blk'), may hold values from 0 to 32767
- donor_weight: float32 [4, 32, 8, 1024], P('sys', 'blk'), may hold values from 0.02 to 0.25
- block_count: int32 [4, 32, 8], P('sys', 'blk'), may hold values from 64 to 128, as said below
Outputs:
- adjoint_next: float32 [4, 8, 5, 512, 16, 128], P('sys', 'inst', None, 'blk')
Inputs may be any that keep to these rules, and one draw needn't show every extreme that they name: `donor_owner`: in the 1024 rows of one block no owner is named by more than 16 rows. `block_count`: the first group of rows of block 0 of system 0 is full.
All inputs are finite; a program needn't handle non-finite values.
Results may differ from a plain program's by a relative error of at most 0.00005.
Values sent between devices are 32-bit elements; how exact they have to be, the bound alone decides.
No kernel may reach another device: no remote copies, remote signals or barrier semaphores. Data moves between devices by JAX's collectives and lax.ppermute only.
A program may use at most 128 MiB of HBM per device.

v0:
```python
import math

import jax
import jax.numpy as jnp
from jax import lax
from jax.experimental import pallas as pl
from jax.experimental.pallas import tpu as pltpu
from jax.sharding import Mesh, PartitionSpec as P

ROTOR_RATE = 0.6
F32 = jnp.float32
BF16 = jnp.bfloat16

FIELDS = 5
INSTANCES = 8
LOCAL = 4
CH = LOCAL * FIELDS
HI = 256
LO = 128
ROWS = 1024
CAP = 16
SLOT = 40
NEAR = 64
PIECE = CAP * SLOT // LO
FIRST = 3
ACCS = 8


def spectra_entry(offset):
    offset %= INSTANCES
    if offset == 0:
        return 0.0
    angle = math.pi * offset / INSTANCES
    return 0.5 * (-1.0) ** offset * math.cos(angle) / math.sin(angle)


def iota(shape, dim):
    return lax.broadcasted_iota(jnp.int32, shape, dim)


def split(x):
    head = x.astype(BF16)
    return head, (x - head.astype(F32)).astype(BF16)


def takes(microseconds):
    return pl.CostEstimate(flops=0, bytes_accessed=microseconds * 3_700_000, transcendentals=0)


def nt_dot(a, b):
    return lax.dot_general(a, b, (((1,), (1,)), ((), ())), preferred_element_type=F32)


def pick_kernel(counts, *refs):
    (cells, *small), (payload, top, bottom) = refs[:5], refs[5:8]
    adj, cell, owner, donor, weight, sem, small_sem = refs[8:]

    def chunk_copy(i):
        here = pl.ds(i * LOCAL, LOCAL)
        return pltpu.make_async_copy(cells.at[here], adj.at[here], sem.at[i])

    copies = [
        pltpu.make_async_copy(operand, place, small_sem.at[i])
        for i, (operand, place) in enumerate(zip(small, (cell, owner, donor, weight)))
    ]
    for copy in copies:
        copy.start()
    for i in range(FIELDS):
        chunk_copy(i).start()
    for copy in copies:
        copy.wait()
    for i in range(FIELDS):
        chunk_copy(i).wait()
    spot = cell[...]
    high = (spot >> 7) & 127
    low = ((spot >> 14) << 7) | (spot & 127)
    lefts = []
    for channel in range(CH):
        whole = adj[channel]
        head, tail = split(jnp.concatenate([whole[:LO], whole[LO:]], axis=1))
        lefts.append(jnp.concatenate([head, tail], axis=1))
    left = jnp.concatenate(lefts, axis=0)
    wide = 256
    for part in range(ROWS // wide):
        cols = slice(part * wide, (part + 1) * wide)
        lows = jnp.where(iota((2 * LO, wide), 0) == low[:, cols], 1.0, 0.0).astype(BF16)
        lows = jnp.concatenate([lows, lows], axis=0)
        here = iota((LO, wide), 0) == high[:, cols]
        found = jnp.dot(left, lows, preferred_element_type=F32)
        for channel in range(CH):
            payload[channel : channel + 1, cols] = jnp.sum(
                jnp.where(here, found[channel * LO : (channel + 1) * LO], 0.0),
                axis=0,
                keepdims=True,
            )
    for group in range(ROWS // LO):
        lanes = slice(group * LO, (group + 1) * LO)
        living = iota((1, LO), 1) < counts[group]
        payload[CH : CH + 1, lanes] = jnp.where(living, owner[:, lanes], -1).astype(F32)
    payload[CH + 1 : 24, :] = jnp.zeros((23 - CH, ROWS), F32)
    payload[24:32, :] = weight[...]
    payload[32:40, :] = donor[...].astype(F32)
    for channel in range(CH):
        top[channel] = adj[channel, HI - 16 :, :]
        bottom[channel] = adj[channel, :16, :]


def pack_kernel(position, own, got, message):
    upto = jnp.where(iota((LO, LO), 0) <= iota((LO, LO), 1), 1.0, 0.0).astype(BF16)
    ones = jnp.ones((LO, LO), BF16)
    for half, payload in enumerate((own, got)):
        rows = payload[...]
        name = rows[CH : CH + 1].astype(jnp.int32)
        near = ((name >> 4) & 1) == position[0]
        name = jnp.where((name >= 0) & near, ((name >> 5) << 4) | (name & 15), -1)
        before = jnp.zeros((NEAR, LO), F32)
        chosen, ranks = [], []
        for group in range(ROWS // LO):
            lanes = slice(group * LO, (group + 1) * LO)
            hit = jnp.where(iota((NEAR, LO), 0) == name[:, lanes], 1.0, 0.0)
            hit16 = hit.astype(BF16)
            count = jnp.dot(hit16, upto, preferred_element_type=F32) + before
            before = before + jnp.dot(hit16, ones, preferred_element_type=F32)
            ranks.append(jnp.sum(hit * count, axis=0, keepdims=True) - 1.0)
            chosen.append(hit16)
        chosen = jnp.concatenate(chosen, axis=1)
        rank = jnp.concatenate(ranks, axis=1)
        placed = jnp.concatenate(
            [jnp.where(rank == float(slot), rows, 0.0) for slot in range(CAP)], axis=0
        )
        head, tail = split(placed)
        table = nt_dot(head, chosen) + nt_dot(tail, chosen)
        for piece in range(PIECE):
            block = table[piece * LO : (piece + 1) * LO].T
            message[pl.ds(half * PIECE + piece, NEAR, stride=2 * PIECE), :] = block


def local_kernel(adj, below, above, gradient, jacobian, coupling, step, out, edge):
    planes = step.shape[0]
    rows = planes * 16
    index = pl.program_id(0)
    last = pl.num_programs(0) - 1
    y = iota((rows, LO), 0) % 16
    z = iota((rows, LO), 1)
    faces = [coupling[d].reshape(rows, LO) for d in range(6)]
    faces[2] = jnp.where(y == 15, 0.0, faces[2])
    faces[3] = jnp.where(y == 0, 0.0, faces[3])
    faces[4] = jnp.where(z == LO - 1, 0.0, faces[4])
    faces[5] = jnp.where(z == 0, 0.0, faces[5])
    tau = step[...].reshape(rows, LO)

    @pl.when(index == 0)
    def _():
        edge[0] = (tau * faces[1])[:16]

    @pl.when(index == last)
    def _():
        edge[1] = (tau * faces[0])[-16:]

    for field in range(FIELDS):
        blocks = [jacobian[g, field].reshape(rows, LO) for g in range(FIELDS)]
        mine = [
            adj[t * FIELDS + field].reshape(rows, LO) for t in range(LOCAL)
        ]
        for t in range(LOCAL):
            channel = t * FIELDS + field
            own = mine[t]
            total = -gradient[channel].reshape(rows, LO)
            for g in range(FIELDS):
                total = total + blocks[g] * adj[t * FIELDS + g].reshape(rows, LO)
            next_plane = jnp.where(index == last, 0.0, above[channel, 0])
            past_plane = jnp.where(index == 0, 0.0, below[channel, 0])
            total = total - faces[0] * jnp.concatenate([own[16:], next_plane], axis=0)
            total = total - faces[1] * jnp.concatenate([past_plane, own[:-16]], axis=0)
            total = total - faces[2] * pltpu.roll(own, rows - 1, 0)
            total = total - faces[3] * pltpu.roll(own, 1, 0)
            total = total - faces[4] * pltpu.roll(own, LO - 1, 1)
            total = total - faces[5] * pltpu.roll(own, 1, 1)
            for s in range(LOCAL):
                if s != t:
                    total = total + (ROTOR_RATE * spectra_entry(s - t)) * mine[s]
            out[channel] = (own - tau * total).reshape(planes, 16, LO)


def fringe_kernel(rows, partial, step, out, *scratch):
    accs = scratch[:ACCS]
    flat, expand, order, places, indices, products, held, sem, held_sem = scratch[ACCS:]
    fetch = pltpu.make_async_copy(partial, held, held_sem)
    fetch.start()
    for piece in range(PIECE):
        flat[pl.ds(piece * LO, LO), :] = rows[pl.ds(piece, LO, stride=PIECE), :].T

    weights = jnp.concatenate(
        [flat[slot * SLOT + 24 : slot * SLOT + 32, :] for slot in range(CAP)], axis=0
    )
    alive = jnp.where(weights > 0.0, 1.0, 0.0)
    upto = jnp.where(iota((LO, LO), 0) <= iota((LO, LO), 1), 1.0, 0.0).astype(BF16)
    rank = jnp.dot(alive.astype(BF16), upto, preferred_element_type=F32) * alive - 1.0
    order[...] = rank.astype(jnp.int32)
    places[LO : LO + 8, :] = nt_dot(jnp.ones((8, LO), BF16), alive.astype(BF16)).astype(jnp.int32)

    def move_of(slot):
        target = order[pl.ds(pl.multiple_of(slot * 8, 8), 1), :]
        return jnp.where(iota((LO, LO), 0) == target, 1.0, 0.0).astype(BF16)

    @pl.loop(0, CAP // 4)
    def _(four):
        for i in range(4):
            slot = four * 4 + i
            spot = flat[pl.ds(pl.multiple_of(slot * SLOT, 8) + 32, 8), :]
            head = spot.astype(BF16).astype(F32)
            both = jnp.concatenate([head, spot - head], axis=0).astype(BF16)
            both = nt_dot(both, move_of(slot))
            spot = (both[:8] + both[8:]).astype(jnp.int32)
            places[pl.ds(pl.multiple_of(slot * 8, 8), 8), :] = ((spot >> 9) << 7) | (spot & 127)

    copy = pltpu.make_async_copy(places, indices, sem)
    copy.start()

    row = iota((LO, LO), 0)
    lane = iota((LO, LO), 1)
    value_row = jnp.where(row < 24, row, row - 24)
    hit = (row < 48) & (value_row == lane // 4)
    expand[:, 0:LO] = jnp.where(hit, 1.0, 0.0).astype(BF16)
    weight_row = jnp.where(row < 80, row - 48, row - 80)
    for k in range(8):
        hit = (row >= 48) & (row < 112) & (weight_row == (lane % 4) * 8 + k)
        expand[:, (k + 1) * LO : (k + 2) * LO] = jnp.where(hit, 1.0, 0.0).astype(BF16)

    @pl.loop(0, CAP // 4)
    def _(four):
        for i in range(4):
            slot = four * 4 + i
            base = pl.multiple_of(slot * SLOT, 8)
            values = flat[pl.ds(base, 24), :]
            weights = flat[pl.ds(base + 24, 8), :]
            quarter = (flat[pl.ds(base + 32, 8), :].astype(jnp.int32) >> 7) & 3
            weights = jnp.concatenate(
                [jnp.where(quarter == q, weights, 0.0) for q in range(4)], axis=0
            )
            values_head = values.astype(BF16).astype(F32)
            weights_head = weights.astype(BF16).astype(F32)
            left = jnp.concatenate(
                [
                    values_head,
                    values - values_head,
                    weights_head,
                    weights - weights_head,
                    jnp.zeros((16, LO), F32),
                ],
                axis=0,
            )
            turned = nt_dot(move_of(slot), left.astype(BF16)).astype(BF16)
            both = jnp.dot(turned, expand[...], preferred_element_type=F32)
            here = pl.ds(pl.multiple_of(slot * LO, LO), LO)
            for k in range(8):
                products[k, here, :] = both[:, 0:LO] * both[:, (k + 1) * LO : (k + 2) * LO]

    zeros = jnp.zeros((64, LO), F32)

    @pl.loop(0, 8192 // 64)
    def _(i):
        for acc in accs:
            acc[pl.ds(pl.multiple_of(i * 64, 64), 64), :] = zeros

    copy.wait()
    listed = indices.reshape((LO + 8) * LO)

    @pl.loop(0, CAP)
    def _(slot):
        unroll = 8

        @pl.loop(0, (listed[LO * LO + slot * 8] + (unroll - 1)) // unroll)
        def _(chunk):
            for u in range(unroll):
                source = chunk * unroll + u
                for k in range(8):
                    acc = accs[k % ACCS]
                    place = listed[slot * 8 * LO + chunk * unroll + (k * LO + u)]
                    acc[pl.ds(place, 1), :] = (
                        acc[pl.ds(place, 1), :] + products[k, pl.ds(slot * LO + source, 1), :]
                    )

    fetch.wait()

    @pl.loop(0, HI // 8, unroll=4)
    def _(i):
        turned = []
        for half in range(2):
            begin = pl.multiple_of(i * 256 + half * LO, LO)
            total = accs[0][pl.ds(begin, LO), :]
            for acc in accs[1:]:
                total = total + acc[pl.ds(begin, LO), :]
            turned.append(total.T)
        here = pl.ds(pl.multiple_of(i * 8, 8), 8)
        tau = step[here, :]
        for channel in range(CH):
            cells = slice(channel * 4, channel * 4 + 4)
            gained = jnp.concatenate([turned[0][cells], turned[1][cells]], axis=0)
            out[channel, here, :] = held[channel, here, :] - tau * gained


def final_kernel(partial, first, rest, step, before, after, edge, out, ready, sem):
    steps = 8
    wide = HI // steps

    def copy_of(i):
        here = pl.ds(pl.multiple_of(i * wide, wide), wide)
        return pltpu.make_async_copy(ready.at[:, here, :], out.at[:, here, :], sem.at[i])

    def block(i):
        here = pl.ds(pl.multiple_of(i * wide, wide), wide)
        tau = step[here, :]
        for field in range(FIELDS):
            channels = [s * FIELDS + field for s in range(LOCAL)]
            others = [
                first[c, here, :] if c < FIRST else rest[c - FIRST, here, :] for c in channels
            ]
            for t in range(LOCAL):
                total = None
                for s in range(LOCAL):
                    if s == t:
                        continue
                    term = (ROTOR_RATE * spectra_entry(s - t + LOCAL)) * others[s]
                    total = term if total is None else total + term
                channel = channels[t]
                ready[channel, here, :] = partial[channel, here, :] - tau * total

    @pl.loop(0, steps)
    def _(i):
        block(i)

        @pl.when(i == 0)
        def _():
            for channel in range(CH):
                ready[channel, :16, :] += edge[0] * before[channel]

        @pl.when(i == steps - 1)
        def _():
            for channel in range(CH):
                ready[channel, HI - 16 :, :] += edge[1] * after[channel]

        copy_of(i).start()

    for i in range(steps):
        copy_of(i).wait()


def shards(
    adjoint,
    gradient,
    jacobian,
    coupling,
    pseudo_step,
    receptor_cell,
    donor_owner,
    donor_cell,
    donor_weight,
    block_count,
):
    swap = [(0, 1), (1, 0)]
    blocks = lax.axis_size("xl") * lax.axis_size("zc")
    cells = adjoint.reshape(CH, HI, LO)
    planes = adjoint.reshape(CH, 16, 16, LO)
    vmem = pl.BlockSpec(memory_space=pltpu.VMEM)
    smem = pl.BlockSpec(memory_space=pltpu.SMEM)
    hbm = pl.BlockSpec(memory_space=pltpu.HBM)

    first = lax.ppermute(cells[:FIRST], "inst", swap)
    payload, top, bottom = pl.pallas_call(
        pick_kernel,
        out_shape=[
            jax.ShapeDtypeStruct((SLOT, ROWS), F32),
            jax.ShapeDtypeStruct((CH, 16, LO), F32),
            jax.ShapeDtypeStruct((CH, 16, LO), F32),
        ],
        in_specs=[smem] + [hbm] * 5,
        out_specs=[vmem] * 3,
        scratch_shapes=[
            pltpu.VMEM((CH, HI, LO), F32),
            pltpu.VMEM((1, ROWS), jnp.int32),
            pltpu.VMEM((1, ROWS), jnp.int32),
            pltpu.VMEM((8, ROWS), jnp.int32),
            pltpu.VMEM((8, ROWS), F32),
            pltpu.SemaphoreType.DMA((FIELDS,)),
            pltpu.SemaphoreType.DMA((4,)),
        ],
        compiler_params=pltpu.CompilerParams(vmem_limit_bytes=56 * 2**20),
        cost_estimate=takes(5),
        name="pick",
    )(
        block_count.reshape(8),
        cells,
        receptor_cell.reshape(1, ROWS),
        donor_owner.reshape(1, ROWS),
        donor_cell.reshape(8, ROWS),
        donor_weight.reshape(8, ROWS),
    )
    got = lax.ppermute(payload, "xl", swap)
    rest, got, first = lax.optimization_barrier((cells[FIRST:], got, first))
    rest = lax.ppermute(rest, "inst", swap)

    message = pl.pallas_call(
        pack_kernel,
        out_shape=jax.ShapeDtypeStruct((NEAR * 2 * PIECE, LO), F32),
        in_specs=[smem, vmem, vmem],
        out_specs=vmem,
        compiler_params=pltpu.CompilerParams(vmem_limit_bytes=32 * 2**20),
        cost_estimate=takes(3),
        name="pack",
    )(lax.axis_index("xl").astype(jnp.int32).reshape(1), payload, got)
    message, gradient, top, bottom = lax.optimization_barrier((message, gradient, top, bottom))
    arrived = lax.all_to_all(
        message.reshape(-1), ("sys", "zc"), split_axis=0, concat_axis=0, tiled=True
    )
    before = lax.ppermute(top, ("xl", "zc"), [(i, i + 1) for i in range(blocks - 1)])
    after = lax.ppermute(bottom, ("xl", "zc"), [(i + 1, i) for i in range(blocks - 1)])

    steps = 4
    wide = 16 // steps
    partial, edge = pl.pallas_call(
        local_kernel,
        grid=(steps,),
        out_shape=[
            jax.ShapeDtypeStruct((CH, 16, 16, LO), F32),
            jax.ShapeDtypeStruct((2, 16, LO), F32),
        ],
        in_specs=[
            pl.BlockSpec((CH, wide, 16, LO), lambda i: (0, i, 0, 0)),
            pl.BlockSpec((CH, 1, 16, LO), lambda i: (0, jnp.maximum(wide * i - 1, 0), 0, 0)),
            pl.BlockSpec((CH, 1, 16, LO), lambda i: (0, jnp.minimum(wide * i + wide, 15), 0, 0)),
            pl.BlockSpec((CH, wide, 16, LO), lambda i: (0, i, 0, 0)),
            pl.BlockSpec((FIELDS, FIELDS, wide, 16, LO), lambda i: (0, 0, i, 0, 0)),
            pl.BlockSpec((6, wide, 16, LO), lambda i: (0, i, 0, 0)),
            pl.BlockSpec((wide, 16, LO), lambda i: (i, 0, 0)),
        ],
        out_specs=[
            pl.BlockSpec((CH, wide, 16, LO), lambda i: (0, i, 0, 0)),
            pl.BlockSpec((2, 16, LO), lambda i: (0, 0, 0)),
        ],
        compiler_params=pltpu.CompilerParams(vmem_limit_bytes=56 * 2**20),
        cost_estimate=takes(6),
        name="local",
    )(
        planes,
        planes,
        planes,
        gradient.reshape(CH, 16, 16, LO),
        jacobian.reshape(FIELDS, FIELDS, 16, 16, LO),
        coupling.reshape(6, 16, 16, LO),
        pseudo_step.reshape(16, 16, LO),
    )

    arrived, partial = lax.optimization_barrier((arrived, partial))
    tau = pseudo_step.reshape(HI, LO)
    partial = pl.pallas_call(
        fringe_kernel,
        out_shape=jax.ShapeDtypeStruct((CH, HI, LO), F32),
        in_specs=[vmem, hbm, vmem],
        out_specs=vmem,
        scratch_shapes=[pltpu.VMEM((8192, LO), F32)] * ACCS
        + [
            pltpu.VMEM((CAP * SLOT, LO), F32),
            pltpu.VMEM((LO, 9 * LO), BF16),
            pltpu.VMEM((LO, LO), jnp.int32),
            pltpu.VMEM((LO + 8, LO), jnp.int32),
            pltpu.SMEM((LO + 8, LO), jnp.int32),
            pltpu.VMEM((8, CAP * LO, LO), F32),
            pltpu.VMEM((CH, HI, LO), F32),
            pltpu.SemaphoreType.DMA,
            pltpu.SemaphoreType.DMA,
        ],
        compiler_params=pltpu.CompilerParams(vmem_limit_bytes=50 * 2**20),
        cost_estimate=takes(25),
        name="fringe",
    )(arrived.reshape(128 * PIECE, LO), partial.reshape(CH, HI, LO), tau)

    result = pl.pallas_call(
        final_kernel,
        out_shape=jax.ShapeDtypeStruct((CH, HI, LO), F32),
        in_specs=[vmem] * 7,
        out_specs=pl.BlockSpec(memory_space=pl.ANY),
        scratch_shapes=[pltpu.VMEM((CH, HI, LO), F32), pltpu.SemaphoreType.DMA((8,))],
        compiler_params=pltpu.CompilerParams(vmem_limit_bytes=40 * 2**20),
        cost_estimate=takes(2),
        name="final",
    )(partial, first, rest, tau, before, after, edge)
    return result.reshape(adjoint.shape)


def solution(mesh):
    fine = Mesh(mesh.devices.reshape(4, 2, 16, 2), ("sys", "xl", "zc", "inst"))
    blk = ("xl", "zc")
    return jax.shard_map(
        shards,
        mesh=fine,
        in_specs=(
            P("sys", "inst", None, blk, None, None),
            P("sys", "inst", None, blk, None, None),
            P("sys", None, None, blk, None, None),
            P("sys", None, blk, None, None),
            P("sys", blk, None, None),
            P("sys", blk, None),
            P("sys", blk, None, None),
            P("sys", blk, None, None),
            P("sys", blk, None, None),
            P("sys", blk, None),
        ),
        out_specs=P("sys", "inst", None, blk, None, None),
        check_vma=False,
    )
```

profile of v0, /device:TPU:8, one launch (start us, length us, event | category | flops | bytes accessed | tf_op | source)
XLA Modules:
  0.0 71.8 jit_solution(544341238653755570)
XLA Ops:
  0.0 0.0 copy-start.3
  0.0 1.2 %slice.9 = f32[3,256,128]{2,1,0:T(8,128)S(1)} slice(f32[20,256,128]{2,1,0:T(8,128)} %bitcast.22), slice={[0:3], [0:256], [0:128]} | slice | bytes 786432 | tf_op jit(solution)/shard_map/slice | solution.py:369
  1.2 3.1 %collective-permute-start.1 = (f32[3,256,128]{2,1,0:T(8,128)S(1)}, f32[3,256,128]{2,1,0:T(8,128)S(1)}, u32[]{:S(2)}, u32[]{:S(2)}) collective-permute-start(f32[3,256,128]{2,1,0:T(8,128)S(1)} %slice.9), channel_id=1, source_target_pairs={{0,1},{1,0},{2,3},{3,2},{4,5},{5,4},{6,7},{7,6},{8,9},{9,8},{10,11... | collective-permute-start | bytes 1179656 | tf_op jit(solution)/shard_map/ppermute | solution.py:369
  4.3 6.5 %pick.1 = (f32[40,1024]{1,0:T(8,128)}, f32[20,16,128]{2,1,0:T(8,128)}, f32[20,16,128]{2,1,0:T(8,128)}) custom-call(s32[8]{0:T(128)} %bitcast.36, f32[20,256,128]{2,1,0:T(8,128)} %bitcast.23, s32[1,1024]{1,0:T(1,128)} %bitcast.34, s32[1,1024]{1,0:T(1,128)} %bitcast.35, s32[8,1024]{1,0:T(8,128)} %bitcast.32, f32[8,1024]{1,0:T(8,128)} %bitcast.33), custom_call_target="tpu_custom_call" | custom-call | bytes 18500000 | tf_op jit(solution)/shard_map/pick/pallas_call | solution.py:370
  10.7 0.0 copy-start.1
  10.8 0.7 collective-permute-start
  11.4 0.0 copy-done.3
  11.4 1.6 %slice.8 = f32[17,256,128]{2,1,0:T(8,128)} slice(f32[20,256,128]{2,1,0:T(8,128)S(1)} %bitcast.27), slice={[3:20], [0:256], [0:128]} | slice | bytes 4456448 | tf_op jit(solution)/shard_map/slice | solution.py:400
  13.0 4.2 %collective-permute-done.got = f32[40,1024]{1,0:T(8,128)S(1)} collective-permute-done((f32[40,1024]{1,0:T(8,128)}, f32[40,1024]{1,0:T(8,128)S(1)}, u32[]{:S(2)}, u32[]{:S(2)}) %collective-permute-start) | collective-permute-done | bytes 163872 | tf_op jit(solution)/shard_map/ppermute | solution.py:399
  17.2 0.0 collective-permute-done.1.first
  17.2 2.0 %collective-permute-start.2 = (f32[17,256,128]{2,1,0:T(8,128)}, f32[17,256,128]{2,1,0:T(8,128)S(1)}, u32[]{:S(2)}, u32[]{:S(2)}) collective-permute-start(f32[17,256,128]{2,1,0:T(8,128)} %slice.8), channel_id=1, source_target_pairs={{0,1},{1,0},{2,3},{3,2},{4,5},{5,4},{6,7},{7,6},{8,9},{9,8},{10,11... | collective-permute-start | bytes 6684680 | tf_op jit(solution)/shard_map/ppermute | solution.py:401
  19.2 0.0 copy-done.1
  19.2 2.8 %pack.1 = f32[640,128]{1,0:T(8,128)} custom-call(s32[1]{0:T(128)} %bitcast.position, f32[40,1024]{1,0:T(8,128)S(1)} %copy-done.1, f32[40,1024]{1,0:T(8,128)S(1)} %collective-permute-done.got), custom_call_target="tpu_custom_call" | custom-call | bytes 11100000 | tf_op jit(solution)/shard_map/pack/pallas_call | solution.py:403
  22.0 12.1 %all-to-all-start = ((f32[64,1280,1]{1,2,0:T(1,128)}), f32[64,1280,1]{1,2,0:T(1,128)S(1)}, u32[]{:S(2)}, u32[]{:S(2)}) async-start(f32[64,1280,1]{1,2,0:T(1,128)} %bitcast.7), calls=%async_computation | async-start | bytes 655360 | tf_op jit(solution)/shard_map/all_to_all | solution.py:413
  34.1 2.1 %collective-permute-start.3 = (f32[20,16,128]{2,1,0:T(8,128)}, f32[20,16,128]{2,1,0:T(8,128)S(1)}, u32[]{:S(2)}, u32[]{:S(2)}) collective-permute-start(f32[20,16,128]{2,1,0:T(8,128)} %get-tuple-element.30), channel_id=1, source_target_pairs={{0,2},{2,4},{4,6},{6,8},{8,10},{10,12},{12,14},{14,16},{16,18},{18... | collective-permute-start | bytes 491528 | tf_op jit(solution)/shard_map/ppermute | solution.py:416
  36.2 1.3 %collective-permute-start.4 = (f32[20,16,128]{2,1,0:T(8,128)}, f32[20,16,128]{2,1,0:T(8,128)S(1)}, u32[]{:S(2)}, u32[]{:S(2)}) collective-permute-start(f32[20,16,128]{2,1,0:T(8,128)} %get-tuple-element.31), channel_id=1, source_target_pairs={{2,0},{4,2},{6,4},{8,6},{10,8},{12,10},{14,12},{16,14},{18,16},{20... | collective-permute-start | bytes 491528 | tf_op jit(solution)/shard_map/ppermute | solution.py:417
  37.5 0.0 copy-start
  37.5 8.1 %local.1 = (f32[20,16,16,128]{3,2,1,0:T(8,128)}, f32[2,16,128]{2,1,0:T(8,128)}) custom-call(f32[20,16,16,128]{3,2,1,0:T(8,128)} %bitcast.24, f32[20,16,16,128]{3,2,1,0:T(8,128)} %bitcast.25, f32[20,16,16,128]{3,2,1,0:T(8,128)} %bitcast.26, f32[20,16,16,128]{3,2,1,0:T(8,128)} %bitcast.29, f32[5,5,16,16,128]{4,3,2,1,0:T(8,128)} %bitcast.28, ...), custom_call_target="tpu_custom_call" | custom-call | bytes 22200000 | tf_op jit(solution)/shard_map/local/pallas_call | solution.py:421
  45.6 1.5 %all-to-all-done = f32[64,1280,1]{1,2,0:T(1,128)S(1)} async-done(((f32[64,1280,1]{1,2,0:T(1,128)}), f32[64,1280,1]{1,2,0:T(1,128)S(1)}, u32[]{:S(2)}, u32[]{:S(2)}) %all-to-all-start) | async-done | bytes 327712 | tf_op jit(solution)/shard_map/all_to_all | solution.py:413
  47.1 0.0 copy-done
  47.2 0.0 copy-start.2
  47.2 16.6 %fringe.1.partial = f32[20,256,128]{2,1,0:T(8,128)S(1)} custom-call(f32[640,128]{1,0:T(8,128)S(1)} %bitcast.18, f32[20,256,128]{2,1,0:T(8,128)} %bitcast.30, f32[256,128]{1,0:T(8,128)S(1)} %bitcast.20), custom_call_target="tpu_custom_call" | custom-call | bytes 92500000 | tf_op jit(solution)/shard_map/fringe/pallas_call | solution.py:456
  63.8 0.0 collective-permute-done.3.before
  63.8 0.0 collective-permute-done.4.after
  63.8 6.4 %collective-permute-done.2.rest = f32[17,256,128]{2,1,0:T(8,128)S(1)} collective-permute-done((f32[17,256,128]{2,1,0:T(8,128)}, f32[17,256,128]{2,1,0:T(8,128)S(1)}, u32[]{:S(2)}, u32[]{:S(2)}) %collective-permute-start.2) | collective-permute-done | bytes 2228256 | tf_op jit(solution)/shard_map/ppermute | solution.py:401
  70.2 0.0 copy-done.2
  70.2 1.6 %final.1 = f32[20,256,128]{2,1,0:T(8,128)} custom-call(f32[20,256,128]{2,1,0:T(8,128)S(1)} %fringe.1.partial, f32[3,256,128]{2,1,0:T(8,128)S(1)} %collective-permute-done.1.first, f32[17,256,128]{2,1,0:T(8,128)S(1)} %collective-permute-done.2.rest, f32[256,128]{1,0:T(8,128)S(1)} %bitcast.21, f32[20,16,128]{2,1,0:T(8,128)S(1)} %collective-permute-done.3.before, ...), custom_call_target="tpu_custom_call" | custom-call | bytes 7400000 | tf_op jit(solution)/shard_map/final/pallas_call | solution.py:478
Async XLA Ops:
  0.0 11.4 %copy-start.3 = (f32[1,4,5,16,16,128]{5,4,3,2,1,0:T(8,128)S(1)}, f32[1,4,5,16,16,128]{5,4,3,2,1,0:T(8,128)}, u32[]{:S(2)}) copy-start(f32[1,4,5,16,16,128]{5,4,3,2,1,0:T(8,128)} %param.10) | copy-start | bytes 7864324
  1.2 16.0 %collective-permute-start.1 = (f32[3,256,128]{2,1,0:T(8,128)S(1)}, f32[3,256,128]{2,1,0:T(8,128)S(1)}, u32[]{:S(2)}, u32[]{:S(2)}) collective-permute-start(f32[3,256,128]{2,1,0:T(8,128)S(1)} %slice.9), channel_id=1, source_target_pairs={{0,1},{1,0},{2,3},{3,2},{4,5},{5,4},{6,7},{7,6},{8,9},{9,8},{10,11... | collective-permute-start | bytes 1179656 | tf_op jit(solution)/shard_map/ppermute | solution.py:369
  10.7 8.5 %copy-start.1 = (f32[40,1024]{1,0:T(8,128)S(1)}, f32[40,1024]{1,0:T(8,128)}, u32[]{:S(2)}) copy-start(f32[40,1024]{1,0:T(8,128)} %get-tuple-element.19.own) | copy-start | bytes 491524
  10.8 6.5 %collective-permute-start = (f32[40,1024]{1,0:T(8,128)}, f32[40,1024]{1,0:T(8,128)S(1)}, u32[]{:S(2)}, u32[]{:S(2)}) collective-permute-start(f32[40,1024]{1,0:T(8,128)} %get-tuple-element.19.own), channel_id=1, source_target_pairs={{0,32},{32,0},{1,33},{33,1},{2,34},{34,2},{3,35},{35,3},{4,36},{36... | collective-permute-start | bytes 491528 | tf_op jit(solution)/shard_map/ppermute | solution.py:399
  17.2 53.0 %collective-permute-start.2 = (f32[17,256,128]{2,1,0:T(8,128)}, f32[17,256,128]{2,1,0:T(8,128)S(1)}, u32[]{:S(2)}, u32[]{:S(2)}) collective-permute-start(f32[17,256,128]{2,1,0:T(8,128)} %slice.8), channel_id=1, source_target_pairs={{0,1},{1,0},{2,3},{3,2},{4,5},{5,4},{6,7},{7,6},{8,9},{9,8},{10,11... | collective-permute-start | bytes 6684680 | tf_op jit(solution)/shard_map/ppermute | solution.py:401
  22.0 25.1 %all-to-all-start = ((f32[64,1280,1]{1,2,0:T(1,128)}), f32[64,1280,1]{1,2,0:T(1,128)S(1)}, u32[]{:S(2)}, u32[]{:S(2)}) async-start(f32[64,1280,1]{1,2,0:T(1,128)} %bitcast.7), calls=%async_computation | async-start | bytes 655360 | tf_op jit(solution)/shard_map/all_to_all | solution.py:413
  34.1 29.6 %collective-permute-start.3 = (f32[20,16,128]{2,1,0:T(8,128)}, f32[20,16,128]{2,1,0:T(8,128)S(1)}, u32[]{:S(2)}, u32[]{:S(2)}) collective-permute-start(f32[20,16,128]{2,1,0:T(8,128)} %get-tuple-element.30), channel_id=1, source_target_pairs={{0,2},{2,4},{4,6},{6,8},{8,10},{10,12},{12,14},{14,16},{16,18},{18... | collective-permute-start | bytes 491528 | tf_op jit(solution)/shard_map/ppermute | solution.py:416
  36.2 27.6 %collective-permute-start.4 = (f32[20,16,128]{2,1,0:T(8,128)}, f32[20,16,128]{2,1,0:T(8,128)S(1)}, u32[]{:S(2)}, u32[]{:S(2)}) collective-permute-start(f32[20,16,128]{2,1,0:T(8,128)} %get-tuple-element.31), channel_id=1, source_target_pairs={{2,0},{4,2},{6,4},{8,6},{10,8},{12,10},{14,12},{16,14},{18,16},{20... | collective-permute-start | bytes 491528 | tf_op jit(solution)/shard_map/ppermute | solution.py:417
  37.5 9.7 %copy-start = (f32[1,16,16,128]{3,2,1,0:T(8,128)S(1)}, f32[1,16,16,128]{3,2,1,0:T(8,128)}, u32[]{:S(2)}) copy-start(f32[1,16,16,128]{3,2,1,0:T(8,128)} %param.14) | copy-start | bytes 393220
  47.2 23.0 %copy-start.2 = (f32[2,16,128]{2,1,0:T(8,128)S(1)}, f32[2,16,128]{2,1,0:T(8,128)}, u32[]{:S(2)}) copy-start(f32[2,16,128]{2,1,0:T(8,128)} %get-tuple-element.32.edge) | copy-start | bytes 49156
where the time goes:
time: 72.1 us; the launch traced here: 71.8 us
  Pallas kernels  35.6 us (49%)
  starting transfers between devices  21.3 us (30%)
  waiting for transfers between devices  12.1 us (17%)
  local copies, waits for them, and re-layouts  2.77 us (4%)
    pallas_call x1, Pallas kernels, shards(): pl.pallas_call(fringe_kernel, out_shape=jax.ShapeDtypeStruct((CH, HI, LO)...  16.6 us
    all_to_all x1, starting transfers between devices, shards(): lax.all_to_all(message.reshape(-1), ('sys', 'zc'), split_axis=0, concat_a...  12.1 us
    pallas_call x1, Pallas kernels, shards(): pl.pallas_call(local_kernel, grid=(steps,), out_shape=[jax.ShapeDtypeStru...  8.14 us
    pallas_call x1, Pallas kernels, shards(): pl.pallas_call(pick_kernel, out_shape=[jax.ShapeDtypeStruct((SLOT, ROWS),...  6.45 us
    ppermute x1, waiting for transfers between devices, shards(): rest = lax.ppermute(rest, 'inst', swap)  6.39 us
    ppermute x1, waiting for transfers between devices, shards(): got = lax.ppermute(payload, 'xl', swap)  4.2 us
    ppermute x1, starting transfers between devices, shards(): first = lax.ppermute(cells[:FIRST], 'inst', swap)  3.11 us
    pallas_call x1, Pallas kernels, shards(): pl.pallas_call(pack_kernel, out_shape=jax.ShapeDtypeStruct((NEAR * 2 * PI...  2.78 us
  transfers between devices with their start and end apart: 6, of which 3 were waited for; matrix products, arithmetic and copies ran while one was open for 2% of the time, Pallas kernels for 47%

commit v1 on v0

--- a/solution.py
+++ b/solution.py
@@ -326,7 +326,7 @@
                 channel = channels[t]
                 ready[channel, here, :] = partial[channel, here, :] - tau * total
 
-    @pl.loop(0, steps)
+    @pl.loop(0, steps, unroll=2)
     def _(i):
         block(i)
 
@@ -416,7 +416,7 @@
     before = lax.ppermute(top, ("xl", "zc"), [(i, i + 1) for i in range(blocks - 1)])
     after = lax.ppermute(bottom, ("xl", "zc"), [(i + 1, i) for i in range(blocks - 1)])
 
-    steps = 4
+    steps = 2
     wide = 16 // steps
     partial, edge = pl.pallas_call(
         local_kernel,

time: 72.1 us -> 72.1 us (level)
  Pallas kernels: 35.6 us -> 39.6 us
  waiting for transfers between devices: 12.1 us -> 8.14 us
    ppermute x1, waiting for transfers between devices: 6.39 us -> 2.59 us  [shards(): rest = lax.ppermute(rest, 'inst', swap)]
    pallas_call x1, Pallas kernels: 16.6 us -> 20.4 us  [shards(): pl.pallas_call(fringe_kernel, out_shape=jax.ShapeDtypeStruct((CH, HI, LO)...]
  transfers between devices with their start and end apart: 6 -> 6, of which waited for: 3 -> 3; matrix products, arithmetic and copies ran while one was open for 2% -> 2% of each run, Pallas kernels for 47% -> 53%
where the time goes in v1:
time: 72.1 us; the launch traced here: 71.8 us
  Pallas kernels  39.6 us (55%)
  starting transfers between devices  21.3 us (30%)
  waiting for transfers between devices  8.14 us (11%)
  local copies, waits for them, and re-layouts  2.77 us (4%)
    pallas_call x1, Pallas kernels, shards(): pl.pallas_call(fringe_kernel, out_shape=jax.ShapeDtypeStruct((CH, HI, LO)...  20.4 us
    all_to_all x1, starting transfers between devices, shards(): lax.all_to_all(message.reshape(-1), ('sys', 'zc'), split_axis=0, concat_a...  12.1 us
    pallas_call x1, Pallas kernels, shards(): pl.pallas_call(local_kernel, grid=(steps,), out_shape=[jax.ShapeDtypeStru...  8.3 us
    pallas_call x1, Pallas kernels, shards(): pl.pallas_call(pick_kernel, out_shape=[jax.ShapeDtypeStruct((SLOT, ROWS),...  6.45 us
    ppermute x1, waiting for transfers between devices, shards(): got = lax.ppermute(payload, 'xl', swap)  4.2 us
    ppermute x1, starting transfers between devices, shards(): first = lax.ppermute(cells[:FIRST], 'inst', swap)  3.11 us
    pallas_call x1, Pallas kernels, shards(): pl.pallas_call(pack_kernel, out_shape=jax.ShapeDtypeStruct((NEAR * 2 * PI...  2.78 us
    ppermute x1, waiting for transfers between devices, shards(): rest = lax.ppermute(rest, 'inst', swap)  2.59 us
  transfers between devices with their start and end apart: 6, of which 3 were waited for; matrix products, arithmetic and copies ran while one was open for 2% of the time, Pallas kernels for 53%

profile of v1, /device:TPU:8, one launch (start us, length us, event | category | flops | bytes accessed | tf_op | source)
XLA Modules:
  0.0 71.8 jit_solution(12395945376094796155)
XLA Ops:
  0.0 0.0 copy-start.3
  0.0 1.2 %slice.9 = f32[3,256,128]{2,1,0:T(8,128)S(1)} slice(f32[20,256,128]{2,1,0:T(8,128)} %bitcast.22), slice={[0:3], [0:256], [0:128]} | slice | bytes 786432 | tf_op jit(solution)/shard_map/slice | solution.py:369
  1.2 3.1 %collective-permute-start.1 = (f32[3,256,128]{2,1,0:T(8,128)S(1)}, f32[3,256,128]{2,1,0:T(8,128)S(1)}, u32[]{:S(2)}, u32[]{:S(2)}) collective-permute-start(f32[3,256,128]{2,1,0:T(8,128)S(1)} %slice.9), channel_id=1, source_target_pairs={{0,1},{1,0},{2,3},{3,2},{4,5},{5,4},{6,7},{7,6},{8,9},{9,8},{10,11... | collective-permute-start | bytes 1179656 | tf_op jit(solution)/shard_map/ppermute | solution.py:369
  4.3 6.5 %pick.1 = (f32[40,1024]{1,0:T(8,128)}, f32[20,16,128]{2,1,0:T(8,128)}, f32[20,16,128]{2,1,0:T(8,128)}) custom-call(s32[8]{0:T(128)} %bitcast.36, f32[20,256,128]{2,1,0:T(8,128)} %bitcast.23, s32[1,1024]{1,0:T(1,128)} %bitcast.34, s32[1,1024]{1,0:T(1,128)} %bitcast.35, s32[8,1024]{1,0:T(8,128)} %bitcast.32, f32[8,1024]{1,0:T(8,128)} %bitcast.33), custom_call_target="tpu_custom_call" | custom-call | bytes 18500000 | tf_op jit(solution)/shard_map/pick/pallas_call | solution.py:370
  10.7 0.0 copy-start.1
  10.8 0.7 collective-permute-start
  11.4 0.0 copy-done.3
  11.4 1.6 %slice.8 = f32[17,256,128]{2,1,0:T(8,128)} slice(f32[20,256,128]{2,1,0:T(8,128)S(1)} %bitcast.27), slice={[3:20], [0:256], [0:128]} | slice | bytes 4456448 | tf_op jit(solution)/shard_map/slice | solution.py:400
  13.0 4.2 %collective-permute-done.got = f32[40,1024]{1,0:T(8,128)S(1)} collective-permute-done((f32[40,1024]{1,0:T(8,128)}, f32[40,1024]{1,0:T(8,128)S(1)}, u32[]{:S(2)}, u32[]{:S(2)}) %collective-permute-start) | collective-permute-done | bytes 163872 | tf_op jit(solution)/shard_map/ppermute | solution.py:399
  17.2 0.0 collective-permute-done.1.first
  17.2 2.0 %collective-permute-start.2 = (f32[17,256,128]{2,1,0:T(8,128)}, f32[17,256,128]{2,1,0:T(8,128)S(1)}, u32[]{:S(2)}, u32[]{:S(2)}) collective-permute-start(f32[17,256,128]{2,1,0:T(8,128)} %slice.8), channel_id=1, source_target_pairs={{0,1},{1,0},{2,3},{3,2},{4,5},{5,4},{6,7},{7,6},{8,9},{9,8},{10,11... | collective-permute-start | bytes 6684680 | tf_op jit(solution)/shard_map/ppermute | solution.py:401
  19.2 0.0 copy-done.1
  19.2 2.8 %pack.1 = f32[640,128]{1,0:T(8,128)} custom-call(s32[1]{0:T(128)} %bitcast.position, f32[40,1024]{1,0:T(8,128)S(1)} %copy-done.1, f32[40,1024]{1,0:T(8,128)S(1)} %collective-permute-done.got), custom_call_target="tpu_custom_call" | custom-call | bytes 11100000 | tf_op jit(solution)/shard_map/pack/pallas_call | solution.py:403
  22.0 12.1 %all-to-all-start = ((f32[64,1280,1]{1,2,0:T(1,128)}), f32[64,1280,1]{1,2,0:T(1,128)S(1)}, u32[]{:S(2)}, u32[]{:S(2)}) async-start(f32[64,1280,1]{1,2,0:T(1,128)} %bitcast.7), calls=%async_computation | async-start | bytes 655360 | tf_op jit(solution)/shard_map/all_to_all | solution.py:413
  34.1 2.1 %collective-permute-start.3 = (f32[20,16,128]{2,1,0:T(8,128)}, f32[20,16,128]{2,1,0:T(8,128)S(1)}, u32[]{:S(2)}, u32[]{:S(2)}) collective-permute-start(f32[20,16,128]{2,1,0:T(8,128)} %get-tuple-element.30), channel_id=1, source_target_pairs={{0,2},{2,4},{4,6},{6,8},{8,10},{10,12},{12,14},{14,16},{16,18},{18... | collective-permute-start | bytes 491528 | tf_op jit(solution)/shard_map/ppermute | solution.py:416
  36.2 1.3 %collective-permute-start.4 = (f32[20,16,128]{2,1,0:T(8,128)}, f32[20,16,128]{2,1,0:T(8,128)S(1)}, u32[]{:S(2)}, u32[]{:S(2)}) collective-permute-start(f32[20,16,128]{2,1,0:T(8,128)} %get-tuple-element.31), channel_id=1, source_target_pairs={{2,0},{4,2},{6,4},{8,6},{10,8},{12,10},{14,12},{16,14},{18,16},{20... | collective-permute-start | bytes 491528 | tf_op jit(solution)/shard_map/ppermute | solution.py:417
  37.5 0.0 copy-start
  37.5 8.3 %local.1 = (f32[20,16,16,128]{3,2,1,0:T(8,128)}, f32[2,16,128]{2,1,0:T(8,128)}) custom-call(f32[20,16,16,128]{3,2,1,0:T(8,128)} %bitcast.24, f32[20,16,16,128]{3,2,1,0:T(8,128)} %bitcast.25, f32[20,16,16,128]{3,2,1,0:T(8,128)} %bitcast.26, f32[20,16,16,128]{3,2,1,0:T(8,128)} %bitcast.29, f32[5,5,16,16,128]{4,3,2,1,0:T(8,128)} %bitcast.28, ...), custom_call_target="tpu_custom_call" | custom-call | bytes 22200000 | tf_op jit(solution)/shard_map/local/pallas_call | solution.py:421
  45.8 1.3 %all-to-all-done = f32[64,1280,1]{1,2,0:T(1,128)S(1)} async-done(((f32[64,1280,1]{1,2,0:T(1,128)}), f32[64,1280,1]{1,2,0:T(1,128)S(1)}, u32[]{:S(2)}, u32[]{:S(2)}) %all-to-all-start) | async-done | bytes 327712 | tf_op jit(solution)/shard_map/all_to_all | solution.py:413
  47.1 0.0 copy-done
  47.2 0.0 copy-start.2
  47.2 20.4 %fringe.1.partial = f32[20,256,128]{2,1,0:T(8,128)S(1)} custom-call(f32[640,128]{1,0:T(8,128)S(1)} %bitcast.18, f32[20,256,128]{2,1,0:T(8,128)} %bitcast.30, f32[256,128]{1,0:T(8,128)S(1)} %bitcast.20), custom_call_target="tpu_custom_call" | custom-call | bytes 92500000 | tf_op jit(solution)/shard_map/fringe/pallas_call | solution.py:456
  67.6 0.0 collective-permute-done.3.before
  67.6 0.0 collective-permute-done.4.after
  67.6 2.6 %collective-permute-done.2.rest = f32[17,256,128]{2,1,0:T(8,128)S(1)} collective-permute-done((f32[17,256,128]{2,1,0:T(8,128)}, f32[17,256,128]{2,1,0:T(8,128)S(1)}, u32[]{:S(2)}, u32[]{:S(2)}) %collective-permute-start.2) | collective-permute-done | bytes 2228256 | tf_op jit(solution)/shard_map/ppermute | solution.py:401
  70.2 0.0 copy-done.2
  70.2 1.6 %final.1 = f32[20,256,128]{2,1,0:T(8,128)} custom-call(f32[20,256,128]{2,1,0:T(8,128)S(1)} %fringe.1.partial, f32[3,256,128]{2,1,0:T(8,128)S(1)} %collective-permute-done.1.first, f32[17,256,128]{2,1,0:T(8,128)S(1)} %collective-permute-done.2.rest, f32[256,128]{1,0:T(8,128)S(1)} %bitcast.21, f32[20,16,128]{2,1,0:T(8,128)S(1)} %collective-permute-done.3.before, ...), custom_call_target="tpu_custom_call" | custom-call | bytes 7400000 | tf_op jit(solution)/shard_map/final/pallas_call | solution.py:478
Async XLA Ops:
  0.0 11.4 %copy-start.3 = (f32[1,4,5,16,16,128]{5,4,3,2,1,0:T(8,128)S(1)}, f32[1,4,5,16,16,128]{5,4,3,2,1,0:T(8,128)}, u32[]{:S(2)}) copy-start(f32[1,4,5,16,16,128]{5,4,3,2,1,0:T(8,128)} %param.10) | copy-start | bytes 7864324
  1.2 16.0 %collective-permute-start.1 = (f32[3,256,128]{2,1,0:T(8,128)S(1)}, f32[3,256,128]{2,1,0:T(8,128)S(1)}, u32[]{:S(2)}, u32[]{:S(2)}) collective-permute-start(f32[3,256,128]{2,1,0:T(8,128)S(1)} %slice.9), channel_id=1, source_target_pairs={{0,1},{1,0},{2,3},{3,2},{4,5},{5,4},{6,7},{7,6},{8,9},{9,8},{10,11... | collective-permute-start | bytes 1179656 | tf_op jit(solution)/shard_map/ppermute | solution.py:369
  10.7 8.5 %copy-start.1 = (f32[40,1024]{1,0:T(8,128)S(1)}, f32[40,1024]{1,0:T(8,128)}, u32[]{:S(2)}) copy-start(f32[40,1024]{1,0:T(8,128)} %get-tuple-element.19.own) | copy-start | bytes 491524
  10.8 6.5 %collective-permute-start = (f32[40,1024]{1,0:T(8,128)}, f32[40,1024]{1,0:T(8,128)S(1)}, u32[]{:S(2)}, u32[]{:S(2)}) collective-permute-start(f32[40,1024]{1,0:T(8,128)} %get-tuple-element.19.own), channel_id=1, source_target_pairs={{0,32},{32,0},{1,33},{33,1},{2,34},{34,2},{3,35},{35,3},{4,36},{36... | collective-permute-start | bytes 491528 | tf_op jit(solution)/shard_map/ppermute | solution.py:399
  17.2 53.0 %collective-permute-start.2 = (f32[17,256,128]{2,1,0:T(8,128)}, f32[17,256,128]{2,1,0:T(8,128)S(1)}, u32[]{:S(2)}, u32[]{:S(2)}) collective-permute-start(f32[17,256,128]{2,1,0:T(8,128)} %slice.8), channel_id=1, source_target_pairs={{0,1},{1,0},{2,3},{3,2},{4,5},{5,4},{6,7},{7,6},{8,9},{9,8},{10,11... | collective-permute-start | bytes 6684680 | tf_op jit(solution)/shard_map/ppermute | solution.py:401
  22.0 25.1 %all-to-all-start = ((f32[64,1280,1]{1,2,0:T(1,128)}), f32[64,1280,1]{1,2,0:T(1,128)S(1)}, u32[]{:S(2)}, u32[]{:S(2)}) async-start(f32[64,1280,1]{1,2,0:T(1,128)} %bitcast.7), calls=%async_computation | async-start | bytes 655360 | tf_op jit(solution)/shard_map/all_to_all | solution.py:413
  34.1 33.4 %collective-permute-start.3 = (f32[20,16,128]{2,1,0:T(8,128)}, f32[20,16,128]{2,1,0:T(8,128)S(1)}, u32[]{:S(2)}, u32[]{:S(2)}) collective-permute-start(f32[20,16,128]{2,1,0:T(8,128)} %get-tuple-element.30), channel_id=1, source_target_pairs={{0,2},{2,4},{4,6},{6,8},{8,10},{10,12},{12,14},{14,16},{16,18},{18... | collective-permute-start | bytes 491528 | tf_op jit(solution)/shard_map/ppermute | solution.py:416
  36.2 31.4 %collective-permute-start.4 = (f32[20,16,128]{2,1,0:T(8,128)}, f32[20,16,128]{2,1,0:T(8,128)S(1)}, u32[]{:S(2)}, u32[]{:S(2)}) collective-permute-start(f32[20,16,128]{2,1,0:T(8,128)} %get-tuple-element.31), channel_id=1, source_target_pairs={{2,0},{4,2},{6,4},{8,6},{10,8},{12,10},{14,12},{16,14},{18,16},{20... | collective-permute-start | bytes 491528 | tf_op jit(solution)/shard_map/ppermute | solution.py:417
  37.5 9.7 %copy-start = (f32[1,16,16,128]{3,2,1,0:T(8,128)S(1)}, f32[1,16,16,128]{3,2,1,0:T(8,128)}, u32[]{:S(2)}) copy-start(f32[1,16,16,128]{3,2,1,0:T(8,128)} %param.14) | copy-start | bytes 393220
  47.2 23.0 %copy-start.2 = (f32[2,16,128]{2,1,0:T(8,128)S(1)}, f32[2,16,128]{2,1,0:T(8,128)}, u32[]{:S(2)}) copy-start(f32[2,16,128]{2,1,0:T(8,128)} %get-tuple-element.32.edge) | copy-start | bytes 49156
